TPU v7x, 32 devices: a whole 2x2x4 slice. The times are simulated.
32 devices in a mesh: req: 2 (over x), vocab: 16 (over z, y, core).
Axes of the slice: x: 2, y: 2, z: 4, core: 2. Of those that a mesh axis runs over, the one named last changes fastest.
Arguments:
- hidden: bfloat16 [512, 2304], P(('req', 'vocab'))
- norm_gain: float32 [2304], replicated, may hold values from 0.5 to 1.5
- head_weight: bfloat16 [2304, 16384], P(None, 'vocab')
- targets: int32 [512], P(('req', 'vocab')), may hold values from 0 to 16383
- counts: int32 [32], P(('req', 'vocab')), may hold values from 5 to 10, as said below
Outputs:
- logprob: float32 [512], P(('req', 'vocab'))
- entropy: float32 [512], P(('req', 'vocab'))
Inputs may be any that keep to these rules, and one draw needn't show every extreme that they name: The scored slots of a device are its first counts slots; some device holds exactly 10.
All inputs are finite; a program needn't handle non-finite values.
Results may differ from a plain program's by a relative error of at most 0.012.
The roundings to bfloat16 on the way count: a program that leaves them out, or rounds other values in their place, can miss the bound.
Values may be sent and summed in bfloat16 or wider, within the bound.
No kernel may reach another device: no remote copies, remote signals or barrier semaphores. Data moves between devices by JAX's collectives and lax.ppermute only.
A program may use at most 64 MiB of HBM per device.

v0:
```python
import functools

import jax
import jax.numpy as jnp
from jax import lax
from jax.experimental import pallas as pl
from jax.experimental.pallas import tpu as pltpu
from jax.sharding import PartitionSpec as P

logit_scale = 256.0 / 2304.0
CAP = 10
HEAD = 8
TAIL = CAP - HEAD
LANES = 128
PER_TILE = HEAD // TAIL
FIELD = 16
VMEM = pl.BlockSpec(memory_space=pltpu.VMEM)
ANY = pl.BlockSpec(memory_space=pl.ANY)
MIB = 1024 * 1024
N_COLS = 256
FETCH = {"all": (0, 1024)}


def moves(n):
    quarter = n // 4
    if n == 16:
        return [(2 * quarter, 0), (quarter, 1), (3 * quarter, 1)], [3, 1]
    return [(k * quarter, 0) for k in (2, 1, 3)], [quarter >> k for k in range(1, quarter.bit_length())]


def move(block, shift, mask, n):
    return lax.ppermute(block, "vocab", [(i, (i + shift) % n ^ mask) for i in range(n)])


def in_hbm(array):
    return pltpu.with_memory_space_constraint(array, pltpu.HBM)


def strip_at(chunks, c):
    tile, place = divmod(c, PER_TILE)
    return slice(TAIL * place, TAIL * place + TAIL), slice((chunks + tile) * LANES, (chunks + tile + 1) * LANES)


def front_kernel(
    hidden_hbm, gain_hbm, targets_hbm, block_ref, hidden_ref, gain_ref, targets_ref, sems
):
    copies = [
        pltpu.make_async_copy(source, target, sems.at[i])
        for i, (source, target) in enumerate(
            [(hidden_hbm, hidden_ref), (gain_hbm, gain_ref), (targets_hbm, targets_ref)]
        )
    ]
    for copy in copies:
        copy.start()
    for copy in copies:
        copy.wait()
    slots, width = hidden_ref.shape
    chunks = width // LANES + 1
    values = hidden_ref[...].astype(jnp.float32)
    square_mean = jnp.sum(values * values, axis=1, keepdims=True) * (1.0 / width)
    gain = gain_ref[...].reshape(1, width)
    normed = (values * lax.rsqrt(square_mean + 1e-05) * gain).astype(jnp.bfloat16)
    lane = lax.broadcasted_iota(jnp.int32, (slots, LANES), 1)
    sub = lax.broadcasted_iota(jnp.int32, (slots, LANES), 0)
    ids = jnp.broadcast_to(targets_ref[...].reshape(1, slots), (slots, slots))
    own = lax.broadcasted_iota(jnp.int32, (slots, slots), 0) == lax.broadcasted_iota(jnp.int32, (slots, slots), 1)
    ids = jnp.sum(jnp.where(own, ids, 0).astype(jnp.float32), axis=1, keepdims=True).astype(jnp.int32)
    ids = jnp.where(lane == 0, lax.shift_right_logical(ids, 8), jnp.where(lane == 1, ids & 255, 0))
    ids = ids.astype(jnp.float32).astype(jnp.bfloat16)
    block_ref[:, :width] = normed[:HEAD]
    block_ref[:, width:width + LANES] = ids[:HEAD]
    for c in range(chunks):
        rows, columns = strip_at(chunks, c)
        chunk = ids if c == chunks - 1 else normed[:, c * LANES:(c + 1) * LANES]
        block_ref[rows, columns] = chunk[HEAD:CAP]


def front(hidden, gain, targets):
    slots, width = hidden.shape
    chunks = width // LANES + 1
    tiles = chunks + -(-chunks // PER_TILE)
    return pl.pallas_call(
        front_kernel,
        out_shape=pltpu.VMEM((HEAD, tiles * LANES), jnp.bfloat16),
        in_specs=[ANY] * 3,
        out_specs=VMEM,
        scratch_shapes=[
            pltpu.VMEM(hidden.shape, hidden.dtype),
            pltpu.VMEM(gain.shape, gain.dtype),
            pltpu.VMEM(targets.shape, targets.dtype),
            pltpu.SemaphoreType.DMA((3,)),
        ],
        compiler_params=pltpu.CompilerParams(vmem_limit_bytes=4 * MIB),
        name="norm_and_pack",
    )(in_hbm(hidden), in_hbm(gain), in_hbm(targets))


def fetch_kernel(first, after_ref, weight_ref, out_ref, sem):
    del after_ref
    copy = pltpu.make_async_copy(weight_ref.at[:, pl.ds(first, out_ref.shape[1])], out_ref, sem)
    copy.start()
    copy.wait()


def fetch(after, weight, first, last):
    shape = (weight.shape[0], last - first)
    return pl.pallas_call(
        functools.partial(fetch_kernel, first),
        out_shape=pltpu.VMEM(shape, weight.dtype),
        in_specs=[ANY] * 2,
        out_specs=VMEM,
        scratch_shapes=[pltpu.SemaphoreType.DMA],
        cost_estimate=pl.CostEstimate(flops=0, bytes_accessed=2 * shape[0] * shape[1], transcendentals=0),
        compiler_params=pltpu.CompilerParams(vmem_limit_bytes=MIB),
        name="fetch_weights",
    )(after, in_hbm(weight))


def unpack_kernel(*refs):
    *blocks, out_ref = refs
    base = len(blocks) * HEAD
    chunks = out_ref.shape[1] // LANES
    for b, ref in enumerate(blocks):
        out_ref[b * HEAD:(b + 1) * HEAD, :] = ref[:, :chunks * LANES]
        for c in range(chunks):
            rows, columns = strip_at(chunks, c)
            out_ref[base + TAIL * b:base + TAIL * (b + 1), c * LANES:(c + 1) * LANES] = ref[rows, columns]


def unpack(blocks, width):
    return pl.pallas_call(
        unpack_kernel,
        out_shape=pltpu.VMEM((len(blocks) * CAP, width + LANES), jnp.bfloat16),
        in_specs=[VMEM] * len(blocks),
        out_specs=VMEM,
        compiler_params=pltpu.CompilerParams(vmem_limit_bytes=4 * MIB),
        name="unpack",
    )(*blocks)


def stats_kernel(owners, near_ref, far_ref, *refs):
    *weight_refs, out_ref, logits_ref = refs
    n = len(owners)
    half = n // 2
    width = near_ref.shape[1] - LANES
    vocab_dev = logits_ref.shape[1]
    m = n * CAP
    me = lax.axis_index("vocab")
    rows = jnp.concatenate([near_ref[:, :width], far_ref[:, :width]], axis=0)
    ids = jnp.concatenate([near_ref[:, width:], far_ref[:, width:]], axis=0).astype(jnp.float32)
    wanted = (ids[:, 0:1] * 256.0 + ids[:, 1:2]).astype(jnp.int32) - me * vocab_dev
    peak, first = None, 0
    for ref in weight_refs:
        for j in range(0, ref.shape[1], N_COLS):
            z = jnp.dot(rows, ref[:, j:j + N_COLS], preferred_element_type=jnp.float32) * logit_scale
            logits_ref[:, first:first + N_COLS] = z
            first += N_COLS
            for k in range(0, N_COLS, LANES):
                part = z[:, k:k + LANES]
                peak = part if peak is None else jnp.maximum(peak, part)
    peak = jnp.max(peak, axis=1, keepdims=True)
    total = jnp.zeros((m, LANES), jnp.float32)
    moment = jnp.zeros((m, LANES), jnp.float32)
    chosen = jnp.zeros((m, LANES), jnp.float32)
    column = lax.broadcasted_iota(jnp.int32, (m, LANES), 1)
    for j in range(0, vocab_dev, LANES):
        z = logits_ref[:, j:j + LANES]
        e = jnp.exp(z - peak)
        total += e
        moment += e * z
        chosen += jnp.where(column == wanted - j, z, 0.0)
    total = jnp.sum(total, axis=1, keepdims=True)
    moment = jnp.sum(moment, axis=1, keepdims=True)
    chosen = jnp.sum(chosen, axis=1, keepdims=True)
    field = lax.shift_right_logical(column, 4)
    table = jnp.where(field == 0, peak, jnp.where(field == 1, total, jnp.where(field == 2, moment, chosen)))
    lane = lax.broadcasted_iota(jnp.int32, (HEAD, LANES), 1) & (FIELD - 1)
    sub = lax.broadcasted_iota(jnp.int32, (HEAD, LANES), 0)
    tail_mask = lane == HEAD + (sub & (TAIL - 1))
    for b in range(n):
        at = (b // half) * half * CAP
        k = b % half
        head = jnp.where(lane == sub, table[at + k * HEAD:at + (k + 1) * HEAD], 0.0)
        first = at + half * HEAD + k * TAIL
        tile, place = first // HEAD * HEAD, first % HEAD
        inside = tail_mask & (sub >= place) & (sub < place + TAIL)
        line = head + jnp.where(inside, table[tile:tile + HEAD], 0.0)
        shift, mask = owners[b]
        to = lax.rem(me + n - shift, n) ^ mask
        out_ref[pl.ds(to, 1), :] = jnp.sum(line, axis=0, keepdims=True)


def row_stats(owners, near, far, weights):
    n = len(owners)
    vocab_dev = sum(weight.shape[1] for weight in weights)
    return pl.pallas_call(
        functools.partial(stats_kernel, owners),
        out_shape=pltpu.VMEM((n, LANES), jnp.float32),
        in_specs=[VMEM] * (2 + len(weights)),
        out_specs=VMEM,
        scratch_shapes=[pltpu.VMEM((n * CAP, vocab_dev), jnp.float32)],
        compiler_params=pltpu.CompilerParams(vmem_limit_bytes=16 * MIB),
        name="row_stats",
    )(near, far, *weights)


def scored_kernel(counts_ref, scored_ref):
    scored_ref[...] = (lax.broadcasted_iota(jnp.int32, scored_ref.shape, 1) < counts_ref[0]).astype(jnp.float32)


def scored_lanes(counts):
    return pl.pallas_call(scored_kernel, out_shape=pltpu.VMEM((HEAD, LANES), jnp.float32), in_specs=[pl.BlockSpec(memory_space=pltpu.SMEM)], out_specs=VMEM, compiler_params=pltpu.CompilerParams(vmem_limit_bytes=MIB), name='scored')(counts)


def finish_kernel(lines_ref, scored_ref, logprob_ref, entropy_ref):
    slots = logprob_ref.shape[0]
    lines = lines_ref[...]
    peak = jnp.max(lines, axis=0, keepdims=True)
    factor = jnp.exp(lines - peak)

    def field(k):
        return pltpu.roll(lines, LANES - FIELD * k, 1)

    total = jnp.sum(field(1) * factor, axis=0, keepdims=True)
    moment = jnp.sum(field(2) * factor, axis=0, keepdims=True)
    chosen = jnp.sum(field(3), axis=0, keepdims=True)
    log_total = jnp.log(total)
    scored = scored_ref[0:1] > 0.0
    logprob = jnp.where(scored, chosen - peak - log_total, 0.0)
    entropy = jnp.where(scored, peak + log_total - moment / total, 0.0)
    logprob_ref[...] = logprob[0, :slots]
    entropy_ref[...] = entropy[0, :slots]


def finish(lines, scored, slots):
    return pl.pallas_call(
        finish_kernel,
        out_shape=(jax.ShapeDtypeStruct((slots,), jnp.float32),) * 2,
        in_specs=[VMEM] * 2,
        out_specs=[VMEM] * 2,
        compiler_params=pltpu.CompilerParams(vmem_limit_bytes=4 * MIB),
        name="finish",
    )(lines, scored)


def on_device(n, hidden, norm_gain, head_weight, targets, counts):
    slots, width = hidden.shape
    block = front(hidden, norm_gain, targets)
    fetched = {}

    def with_fetch(place, after, value):
        if place not in FETCH:
            return value
        first, last = FETCH[place]
        fetched[place], value = lax.optimization_barrier((fetch(after, head_weight, first, last), value))
        return value

    shifts, masks = moves(n)
    blocks = [block] + [move(block, shift, mask, n) for shift, mask in shifts]
    owners = [(0, 0)] + shifts
    for mask in masks[:-1]:
        blocks = blocks + [move(b, 0, mask, n) for b in blocks]
        owners = owners + [(s, m ^ mask) for s, m in owners]
    blocks = list(with_fetch("all", blocks[len(blocks) // 2 - 1], tuple(blocks)))
    near = unpack(blocks, width)
    far = with_fetch("core", near, move(near, 0, masks[-1], n))
    far, scored = lax.optimization_barrier((far, scored_lanes(counts)))
    owners = owners + [(s, m ^ masks[-1]) for s, m in owners]
    weights = [fetched[place] for place in sorted(fetched, key=lambda place: FETCH[place])]
    lines = row_stats(tuple(owners), near, far, weights)
    lines = lax.all_to_all(lines, "vocab", 0, 0, tiled=True)
    return finish(lines, scored, slots)


def solution(mesh):
    n = mesh.shape["vocab"]
    in_specs = (
        P(("req", "vocab"), None),
        P(),
        P(None, "vocab"),
        P(("req", "vocab")),
        P(("req", "vocab")),
    )
    out_specs = (P(("req", "vocab")), P(("req", "vocab")))

    def step(*args):
        return on_device(n, *args)

    return jax.shard_map(step, mesh=mesh, in_specs=in_specs, out_specs=out_specs, check_vma=False)
```

profile of v0, /device:TPU:0, one launch (start us, length us, event | category | flops | bytes accessed | tf_op | source)
XLA Modules:
  0.0 29.4 jit_solution(3624419453249013923)
XLA Ops:
  0.6 1.0 %norm_and_pack.1.refs_0_ = bf16[8,3072]{1,0:T(8,128)(2,1)S(1)} custom-call(bf16[16,2304]{1,0:T(8,128)(2,1)} %hidden_hbm.1, f32[2304]{0:T(1024)} %gain_hbm.1, s32[16]{0:T(128)} %targets_hbm.1), custom_call_target="tpu_custom_call" | custom-call | tf_op jit(solution)/shard_map/norm_and_pack/pallas_call | solution.py:82
  1.7 2.5 %collective-permute-start.2 = (bf16[8,3072]{1,0:T(8,128)(2,1)S(1)}, bf16[8,3072]{1,0:T(8,128)(2,1)S(1)}, u32[]{:S(2)}, u32[]{:S(2)}) collective-permute-start(bf16[8,3072]{1,0:T(8,128)(2,1)S(1)} %norm_and_pack.1.refs_0_), channel_id=1, source_target_pairs={{0,5},{1,4},{2,7},{3,6},{4,9},{5,8},{6,11},{7,10},{8,13},{9,12},{1... | collective-permute-start | bytes 147464 | tf_op jit(solution)/shard_map/ppermute | solution.py:32
  4.2 2.6 %collective-permute-start.1 = (bf16[8,3072]{1,0:T(8,128)(2,1)S(1)}, bf16[8,3072]{1,0:T(8,128)(2,1)S(1)}, u32[]{:S(2)}, u32[]{:S(2)}) collective-permute-start(bf16[8,3072]{1,0:T(8,128)(2,1)S(1)} %norm_and_pack.1.refs_0_), channel_id=1, source_target_pairs={{0,8},{1,9},{2,10},{3,11},{4,12},{5,13},{6,14},{7,15},{8,0},{9,1},... | collective-permute-start | bytes 147464 | tf_op jit(solution)/shard_map/ppermute | solution.py:32
  6.8 1.4 %collective-permute-start = (bf16[8,3072]{1,0:T(8,128)(2,1)S(1)}, bf16[8,3072]{1,0:T(8,128)(2,1)S(1)}, u32[]{:S(2)}, u32[]{:S(2)}) collective-permute-start(bf16[8,3072]{1,0:T(8,128)(2,1)S(1)} %norm_and_pack.1.refs_0_), channel_id=1, source_target_pairs={{0,13},{1,12},{2,15},{3,14},{4,1},{5,0},{6,3},{7,2},{8,5},{9,4},{1... | collective-permute-start | bytes 147464 | tf_op jit(solution)/shard_map/ppermute | solution.py:32
  8.2 1.2 %collective-permute-start.3 = (bf16[8,3072]{1,0:T(8,128)(2,1)S(1)}, bf16[8,3072]{1,0:T(8,128)(2,1)S(1)}, u32[]{:S(2)}, u32[]{:S(2)}) collective-permute-start(bf16[8,3072]{1,0:T(8,128)(2,1)S(1)} %norm_and_pack.1.refs_0_), channel_id=1, source_target_pairs={{0,3},{1,2},{2,1},{3,0},{4,7},{5,6},{6,5},{7,4},{8,11},{9,10},{10,... | collective-permute-start | bytes 147464 | tf_op jit(solution)/shard_map/ppermute | solution.py:32
  9.4 0.0 collective-permute-done.2.refs_2_
  9.4 0.7 %collective-permute-start.5 = (bf16[8,3072]{1,0:T(8,128)(2,1)S(1)}, bf16[8,3072]{1,0:T(8,128)(2,1)S(1)}, u32[]{:S(2)}, u32[]{:S(2)}) collective-permute-start(bf16[8,3072]{1,0:T(8,128)(2,1)S(1)} %collective-permute-done.2.refs_2_), channel_id=1, source_target_pairs={{0,3},{1,2},{2,1},{3,0},{4,7},{5,6},{6,5},{7,4},{8,11},{9,10},{10,... | collective-permute-start | bytes 147464 | tf_op jit(solution)/shard_map/ppermute | solution.py:32
  10.0 1.0 %collective-permute-done.1.refs_1_ = bf16[8,3072]{1,0:T(8,128)(2,1)S(1)} collective-permute-done((bf16[8,3072]{1,0:T(8,128)(2,1)S(1)}, bf16[8,3072]{1,0:T(8,128)(2,1)S(1)}, u32[]{:S(2)}, u32[]{:S(2)}) %collective-permute-start.1) | collective-permute-done | bytes 49184 | tf_op jit(solution)/shard_map/ppermute | solution.py:32
  11.1 1.3 %collective-permute-start.4 = (bf16[8,3072]{1,0:T(8,128)(2,1)S(1)}, bf16[8,3072]{1,0:T(8,128)(2,1)S(1)}, u32[]{:S(2)}, u32[]{:S(2)}) collective-permute-start(bf16[8,3072]{1,0:T(8,128)(2,1)S(1)} %collective-permute-done.1.refs_1_), channel_id=1, source_target_pairs={{0,3},{1,2},{2,1},{3,0},{4,7},{5,6},{6,5},{7,4},{8,11},{9,10},{10,... | collective-permute-start | bytes 147464 | tf_op jit(solution)/shard_map/ppermute | solution.py:32
  12.3 0.0 collective-permute-done.after_ref.refs_3_
  12.3 0.5 %collective-permute-start.6 = (bf16[8,3072]{1,0:T(8,128)(2,1)S(1)}, bf16[8,3072]{1,0:T(8,128)(2,1)S(1)}, u32[]{:S(2)}, u32[]{:S(2)}) collective-permute-start(bf16[8,3072]{1,0:T(8,128)(2,1)S(1)} %collective-permute-done.after_ref.refs_3_), channel_id=1, source_target_pairs={{0,3},{1,2},{2,1},{3,0},{4,7},{5,6},{6,5},{7,4},{8,11},{9,10},{10,... | collective-permute-start | bytes 147464 | tf_op jit(solution)/shard_map/ppermute | solution.py:32
  12.8 2.3 %fetch_weights.1.refs_0_ = bf16[2304,1024]{1,0:T(8,128)(2,1)S(1)} custom-call(bf16[8,3072]{1,0:T(8,128)(2,1)S(1)} %collective-permute-done.after_ref.refs_3_, bf16[2304,1024]{1,0:T(8,128)(2,1)} %weight_ref.1), custom_call_target="tpu_custom_call" | custom-call | bytes 4718592 | tf_op jit(solution)/shard_map/fetch_weights/pallas_call | solution.py:107
  15.2 0.0 collective-permute-done.3.refs_4_
  15.2 0.0 collective-permute-done.5.refs_6_
  15.2 0.0 collective-permute-done.4.refs_5_
  15.2 0.7 %collective-permute-done.6.refs_7_ = bf16[8,3072]{1,0:T(8,128)(2,1)S(1)} collective-permute-done((bf16[8,3072]{1,0:T(8,128)(2,1)S(1)}, bf16[8,3072]{1,0:T(8,128)(2,1)S(1)}, u32[]{:S(2)}, u32[]{:S(2)}) %collective-permute-start.6) | collective-permute-done | bytes 49184 | tf_op jit(solution)/shard_map/ppermute | solution.py:32
  15.9 0.1 unpack.1.near_ref
  15.9 0.6 %collective-permute-start.7 = (bf16[80,2432]{1,0:T(8,128)(2,1)S(1)}, bf16[80,2432]{1,0:T(8,128)(2,1)S(1)}, u32[]{:S(2)}, u32[]{:S(2)}) collective-permute-start(bf16[80,2432]{1,0:T(8,128)(2,1)S(1)} %unpack.1.near_ref), channel_id=1, source_target_pairs={{0,1},{1,0},{2,3},{3,2},{4,5},{5,4},{6,7},{7,6},{8,9},{9,8},{10,11... | collective-permute-start | bytes 1167368 | tf_op jit(solution)/shard_map/ppermute | solution.py:32
  17.2 0.7 %collective-permute-done.7.far_ref = bf16[80,2432]{1,0:T(8,128)(2,1)S(1)} collective-permute-done((bf16[80,2432]{1,0:T(8,128)(2,1)S(1)}, bf16[80,2432]{1,0:T(8,128)(2,1)S(1)}, u32[]{:S(2)}, u32[]{:S(2)}) %collective-permute-start.7) | collective-permute-done | bytes 389152 | tf_op jit(solution)/shard_map/ppermute | solution.py:32
  17.9 1.3 %row_stats.1 = f32[16,128]{1,0:T(8,128)S(1)} custom-call(bf16[80,2432]{1,0:T(8,128)(2,1)S(1)} %unpack.1.near_ref, bf16[80,2432]{1,0:T(8,128)(2,1)S(1)} %collective-permute-done.7.far_ref, bf16[2304,1024]{1,0:T(8,128)(2,1)S(1)} %fetch_weights.1.refs_0_), custom_call_target="tpu_custom_call" | custom-call | tf_op jit(solution)/shard_map/row_stats/pallas_call | solution.py:196
  19.2 9.6 %all_to_all.11 = f32[16,1,128]{2,1,0:T(1,128)S(1)} all-to-all(f32[16,1,128]{2,1,0:T(1,128)S(1)} %bitcast.4), channel_id=1, replica_groups=mesh['req'=2,'vocab'=16] {'vocab'}, dimensions={0} | all-to-all | bytes 16384 | tf_op jit(solution)/shard_map/all_to_all | solution.py:271
  28.8 0.6 %finish.1 = (f32[16]{0:T(128)}, f32[16]{0:T(128)}) custom-call(f32[16,128]{1,0:T(8,128)S(1)} %bitcast.5, f32[8,128]{1,0:T(8,128)S(1)} %scored.1.scored_ref), custom_call_target="tpu_custom_call" | custom-call | tf_op jit(solution)/shard_map/finish/pallas_call | solution.py:236
  (1 shorter events, 0.0 us)
Async XLA Ops:
  1.7 7.7 %collective-permute-start.2 = (bf16[8,3072]{1,0:T(8,128)(2,1)S(1)}, bf16[8,3072]{1,0:T(8,128)(2,1)S(1)}, u32[]{:S(2)}, u32[]{:S(2)}) collective-permute-start(bf16[8,3072]{1,0:T(8,128)(2,1)S(1)} %norm_and_pack.1.refs_0_), channel_id=1, source_target_pairs={{0,5},{1,4},{2,7},{3,6},{4,9},{5,8},{6,11},{7,10},{8,13},{9,12},{1... | collective-permute-start | bytes 147464 | tf_op jit(solution)/shard_map/ppermute | solution.py:32
  4.2 6.9 %collective-permute-start.1 = (bf16[8,3072]{1,0:T(8,128)(2,1)S(1)}, bf16[8,3072]{1,0:T(8,128)(2,1)S(1)}, u32[]{:S(2)}, u32[]{:S(2)}) collective-permute-start(bf16[8,3072]{1,0:T(8,128)(2,1)S(1)} %norm_and_pack.1.refs_0_), channel_id=1, source_target_pairs={{0,8},{1,9},{2,10},{3,11},{4,12},{5,13},{6,14},{7,15},{8,0},{9,1},... | collective-permute-start | bytes 147464 | tf_op jit(solution)/shard_map/ppermute | solution.py:32
  6.8 5.6 %collective-permute-start = (bf16[8,3072]{1,0:T(8,128)(2,1)S(1)}, bf16[8,3072]{1,0:T(8,128)(2,1)S(1)}, u32[]{:S(2)}, u32[]{:S(2)}) collective-permute-start(bf16[8,3072]{1,0:T(8,128)(2,1)S(1)} %norm_and_pack.1.refs_0_), channel_id=1, source_target_pairs={{0,13},{1,12},{2,15},{3,14},{4,1},{5,0},{6,3},{7,2},{8,5},{9,4},{1... | collective-permute-start | bytes 147464 | tf_op jit(solution)/shard_map/ppermute | solution.py:32
  8.2 7.0 %collective-permute-start.3 = (bf16[8,3072]{1,0:T(8,128)(2,1)S(1)}, bf16[8,3072]{1,0:T(8,128)(2,1)S(1)}, u32[]{:S(2)}, u32[]{:S(2)}) collective-permute-start(bf16[8,3072]{1,0:T(8,128)(2,1)S(1)} %norm_and_pack.1.refs_0_), channel_id=1, source_target_pairs={{0,3},{1,2},{2,1},{3,0},{4,7},{5,6},{6,5},{7,4},{8,11},{9,10},{10,... | collective-permute-start | bytes 147464 | tf_op jit(solution)/shard_map/ppermute | solution.py:32
  9.4 5.8 %collective-permute-start.5 = (bf16[8,3072]{1,0:T(8,128)(2,1)S(1)}, bf16[8,3072]{1,0:T(8,128)(2,1)S(1)}, u32[]{:S(2)}, u32[]{:S(2)}) collective-permute-start(bf16[8,3072]{1,0:T(8,128)(2,1)S(1)} %collective-permute-done.2.refs_2_), channel_id=1, source_target_pairs={{0,3},{1,2},{2,1},{3,0},{4,7},{5,6},{6,5},{7,4},{8,11},{9,10},{10,... | collective-permute-start | bytes 147464 | tf_op jit(solution)/shard_map/ppermute | solution.py:32
  11.1 4.1 %collective-permute-start.4 = (bf16[8,3072]{1,0:T(8,128)(2,1)S(1)}, bf16[8,3072]{1,0:T(8,128)(2,1)S(1)}, u32[]{:S(2)}, u32[]{:S(2)}) collective-permute-start(bf16[8,3072]{1,0:T(8,128)(2,1)S(1)} %collective-permute-done.1.refs_1_), channel_id=1, source_target_pairs={{0,3},{1,2},{2,1},{3,0},{4,7},{5,6},{6,5},{7,4},{8,11},{9,10},{10,... | collective-permute-start | bytes 147464 | tf_op jit(solution)/shard_map/ppermute | solution.py:32
  12.3 3.5 %collective-permute-start.6 = (bf16[8,3072]{1,0:T(8,128)(2,1)S(1)}, bf16[8,3072]{1,0:T(8,128)(2,1)S(1)}, u32[]{:S(2)}, u32[]{:S(2)}) collective-permute-start(bf16[8,3072]{1,0:T(8,128)(2,1)S(1)} %collective-permute-done.after_ref.refs_3_), channel_id=1, source_target_pairs={{0,3},{1,2},{2,1},{3,0},{4,7},{5,6},{6,5},{7,4},{8,11},{9,10},{10,... | collective-permute-start | bytes 147464 | tf_op jit(solution)/shard_map/ppermute | solution.py:32
  15.9 1.9 %collective-permute-start.7 = (bf16[80,2432]{1,0:T(8,128)(2,1)S(1)}, bf16[80,2432]{1,0:T(8,128)(2,1)S(1)}, u32[]{:S(2)}, u32[]{:S(2)}) collective-permute-start(bf16[80,2432]{1,0:T(8,128)(2,1)S(1)} %unpack.1.near_ref), channel_id=1, source_target_pairs={{0,1},{1,0},{2,3},{3,2},{4,5},{5,4},{6,7},{7,6},{8,9},{9,8},{10,11... | collective-permute-start | bytes 1167368 | tf_op jit(solution)/shard_map/ppermute | solution.py:32
where the time goes:
time: 29.6 us; the launch traced here: 29.4 us
  starting transfers between devices  10.7 us (36%)
  blocking collectives  9.63 us (33%)
  Pallas kernels  5.35 us (18%)
  waiting for transfers between devices  2.38 us (8%)
  between operations  1.35 us (5%)
    ppermute x8, starting transfers between devices, move(): lax.ppermute(block, 'vocab', [(i, (i + shift) % n ^ mask) for i in range(...  10.7 us
    all_to_all x1, blocking collectives, on_device(): lines = lax.all_to_all(lines, 'vocab', 0, 0, tiled=True)  9.63 us
    ppermute x8, waiting for transfers between devices, move(): lax.ppermute(block, 'vocab', [(i, (i + shift) % n ^ mask) for i in range(...  2.38 us
    pallas_call x1, Pallas kernels, fetch(): pl.pallas_call(functools.partial(fetch_kernel, first), out_shape=pltpu.VM...  2.34 us
    pallas_call x1, Pallas kernels, row_stats(): pl.pallas_call(functools.partial(stats_kernel, owners), out_shape=pltpu.V...  1.28 us
    pallas_call x1, Pallas kernels, front(): pl.pallas_call(front_kernel, out_shape=pltpu.VMEM((HEAD, tiles * LANES),...  1.03 us
    pallas_call x1, Pallas kernels, finish(): pl.pallas_call(finish_kernel, out_shape=(jax.ShapeDtypeStruct((slots,), j...  0.6 us
  transfers between devices with their start and end apart: 8, of which 3 were waited for; matrix products, arithmetic and copies ran while one was open for 0% of the time, Pallas kernels for 8%

commit v1 on v0

--- a/solution.py
+++ b/solution.py
@@ -18,14 +18,14 @@
 ANY = pl.BlockSpec(memory_space=pl.ANY)
 MIB = 1024 * 1024
 N_COLS = 256
-FETCH = {"all": (0, 1024)}
+ROWS_STEP = 128
 
 
 def moves(n):
     quarter = n // 4
     if n == 16:
-        return [(2 * quarter, 0), (quarter, 1), (3 * quarter, 1)], [3, 1]
-    return [(k * quarter, 0) for k in (2, 1, 3)], [quarter >> k for k in range(1, quarter.bit_length())]
+        return [(quarter, 1), (2 * quarter, 0), (3 * quarter, 1)], [3, 1]
+    return [(k * quarter, 0) for k in (1, 2, 3)], [quarter >> k for k in range(1, quarter.bit_length())]
 
 
 def move(block, shift, mask, n):
@@ -95,22 +95,21 @@
     )(in_hbm(hidden), in_hbm(gain), in_hbm(targets))
 
 
-def fetch_kernel(first, after_ref, weight_ref, out_ref, sem):
+def fetch_kernel(after_ref, weight_ref, out_ref, sem):
     del after_ref
-    copy = pltpu.make_async_copy(weight_ref.at[:, pl.ds(first, out_ref.shape[1])], out_ref, sem)
+    copy = pltpu.make_async_copy(weight_ref, out_ref, sem)
     copy.start()
     copy.wait()
 
 
-def fetch(after, weight, first, last):
-    shape = (weight.shape[0], last - first)
-    return pl.pallas_call(
-        functools.partial(fetch_kernel, first),
-        out_shape=pltpu.VMEM(shape, weight.dtype),
+def fetch(after, weight):
+    return pl.pallas_call(
+        fetch_kernel,
+        out_shape=pltpu.VMEM(weight.shape, weight.dtype),
         in_specs=[ANY] * 2,
         out_specs=VMEM,
         scratch_shapes=[pltpu.SemaphoreType.DMA],
-        cost_estimate=pl.CostEstimate(flops=0, bytes_accessed=2 * shape[0] * shape[1], transcendentals=0),
+        cost_estimate=pl.CostEstimate(flops=0, bytes_accessed=2 * weight.size, transcendentals=0),
         compiler_params=pltpu.CompilerParams(vmem_limit_bytes=MIB),
         name="fetch_weights",
     )(after, in_hbm(weight))
@@ -138,33 +137,34 @@
     )(*blocks)
 
 
-def stats_kernel(owners, near_ref, far_ref, *refs):
-    *weight_refs, out_ref, logits_ref = refs
-    n = len(owners)
-    half = n // 2
-    width = near_ref.shape[1] - LANES
+def stats_kernel(n, owners, rows_in, weight_ref, out_ref, logits_ref):
+    count = len(owners)
+    width = rows_in.shape[1] - LANES
     vocab_dev = logits_ref.shape[1]
-    m = n * CAP
+    used, m = rows_in.shape[0], logits_ref.shape[0]
     me = lax.axis_index("vocab")
-    rows = jnp.concatenate([near_ref[:, :width], far_ref[:, :width]], axis=0)
-    ids = jnp.concatenate([near_ref[:, width:], far_ref[:, width:]], axis=0).astype(jnp.float32)
+    rows, ids = rows_in[:, :width], rows_in[:, width:]
+    if m > used:
+        rows = jnp.concatenate([rows, jnp.zeros((m - used, width), rows.dtype)], axis=0)
+        ids = jnp.concatenate([ids, jnp.zeros((m - used, LANES), ids.dtype)], axis=0)
+    ids = ids.astype(jnp.float32)
     wanted = (ids[:, 0:1] * 256.0 + ids[:, 1:2]).astype(jnp.int32) - me * vocab_dev
-    peak, first = None, 0
-    for ref in weight_refs:
-        for j in range(0, ref.shape[1], N_COLS):
-            z = jnp.dot(rows, ref[:, j:j + N_COLS], preferred_element_type=jnp.float32) * logit_scale
-            logits_ref[:, first:first + N_COLS] = z
-            first += N_COLS
-            for k in range(0, N_COLS, LANES):
-                part = z[:, k:k + LANES]
-                peak = part if peak is None else jnp.maximum(peak, part)
-    peak = jnp.max(peak, axis=1, keepdims=True)
+    peak = None
+    for j in range(0, vocab_dev, N_COLS):
+        z = jnp.dot(rows, weight_ref[:, j:j + N_COLS], preferred_element_type=jnp.float32) * logit_scale
+        logits_ref[:, j:j + N_COLS] = z
+        for k in range(0, N_COLS, LANES):
+            part = z[:, k:k + LANES]
+            peak = part if peak is None else jnp.maximum(peak, part)
+    m = used
+    peak = jnp.max(peak[:m], axis=1, keepdims=True)
+    wanted = wanted[:m]
     total = jnp.zeros((m, LANES), jnp.float32)
     moment = jnp.zeros((m, LANES), jnp.float32)
     chosen = jnp.zeros((m, LANES), jnp.float32)
     column = lax.broadcasted_iota(jnp.int32, (m, LANES), 1)
     for j in range(0, vocab_dev, LANES):
-        z = logits_ref[:, j:j + LANES]
+        z = logits_ref[:m, j:j + LANES]
         e = jnp.exp(z - peak)
         total += e
         moment += e * z
@@ -177,12 +177,10 @@
     lane = lax.broadcasted_iota(jnp.int32, (HEAD, LANES), 1) & (FIELD - 1)
     sub = lax.broadcasted_iota(jnp.int32, (HEAD, LANES), 0)
     tail_mask = lane == HEAD + (sub & (TAIL - 1))
-    for b in range(n):
-        at = (b // half) * half * CAP
-        k = b % half
-        head = jnp.where(lane == sub, table[at + k * HEAD:at + (k + 1) * HEAD], 0.0)
-        first = at + half * HEAD + k * TAIL
-        tile, place = first // HEAD * HEAD, first % HEAD
+    for b in range(count):
+        head = jnp.where(lane == sub, table[b * HEAD:(b + 1) * HEAD], 0.0)
+        at = count * HEAD + b * TAIL
+        tile, place = at // HEAD * HEAD, at % HEAD
         inside = tail_mask & (sub >= place) & (sub < place + TAIL)
         line = head + jnp.where(inside, table[tile:tile + HEAD], 0.0)
         shift, mask = owners[b]
@@ -190,18 +188,25 @@
         out_ref[pl.ds(to, 1), :] = jnp.sum(line, axis=0, keepdims=True)
 
 
-def row_stats(owners, near, far, weights):
-    n = len(owners)
-    vocab_dev = sum(weight.shape[1] for weight in weights)
-    return pl.pallas_call(
-        functools.partial(stats_kernel, owners),
+def more_stats_kernel(n, owners, rows_in, weight_ref, lines_in, out_ref, logits_ref):
+    del lines_in
+    stats_kernel(n, owners, rows_in, weight_ref, out_ref, logits_ref)
+
+
+def row_stats(n, owners, rows, weight, lines=None):
+    vocab_dev = weight.shape[1]
+    more = lines is not None
+    return pl.pallas_call(
+        functools.partial(more_stats_kernel if more else stats_kernel, n, owners),
         out_shape=pltpu.VMEM((n, LANES), jnp.float32),
-        in_specs=[VMEM] * (2 + len(weights)),
-        out_specs=VMEM,
-        scratch_shapes=[pltpu.VMEM((n * CAP, vocab_dev), jnp.float32)],
+        in_specs=[VMEM] * 2 + [ANY] * more,
+        out_specs=VMEM,
+        input_output_aliases={2: 0} if more else {},
+        scratch_shapes=[pltpu.VMEM((-(-rows.shape[0] // ROWS_STEP) * ROWS_STEP, vocab_dev), jnp.float32)],
+        cost_estimate=pl.CostEstimate(flops=2 * rows.size * vocab_dev, bytes_accessed=0, transcendentals=0),
         compiler_params=pltpu.CompilerParams(vmem_limit_bytes=16 * MIB),
         name="row_stats",
-    )(near, far, *weights)
+    )(rows, weight, *([lines] if more else []))
 
 
 def scored_kernel(counts_ref, scored_ref):
@@ -209,7 +214,14 @@
 
 
 def scored_lanes(counts):
-    return pl.pallas_call(scored_kernel, out_shape=pltpu.VMEM((HEAD, LANES), jnp.float32), in_specs=[pl.BlockSpec(memory_space=pltpu.SMEM)], out_specs=VMEM, compiler_params=pltpu.CompilerParams(vmem_limit_bytes=MIB), name='scored')(counts)
+    return pl.pallas_call(
+        scored_kernel,
+        out_shape=pltpu.VMEM((HEAD, LANES), jnp.float32),
+        in_specs=[pl.BlockSpec(memory_space=pltpu.SMEM)],
+        out_specs=VMEM,
+        compiler_params=pltpu.CompilerParams(vmem_limit_bytes=MIB),
+        name="scored",
+    )(counts)
 
 
 def finish_kernel(lines_ref, scored_ref, logprob_ref, entropy_ref):
@@ -246,28 +258,19 @@
 def on_device(n, hidden, norm_gain, head_weight, targets, counts):
     slots, width = hidden.shape
     block = front(hidden, norm_gain, targets)
-    fetched = {}
-
-    def with_fetch(place, after, value):
-        if place not in FETCH:
-            return value
-        first, last = FETCH[place]
-        fetched[place], value = lax.optimization_barrier((fetch(after, head_weight, first, last), value))
-        return value
-
     shifts, masks = moves(n)
     blocks = [block] + [move(block, shift, mask, n) for shift, mask in shifts]
     owners = [(0, 0)] + shifts
     for mask in masks[:-1]:
         blocks = blocks + [move(b, 0, mask, n) for b in blocks]
         owners = owners + [(s, m ^ mask) for s, m in owners]
-    blocks = list(with_fetch("all", blocks[len(blocks) // 2 - 1], tuple(blocks)))
+    beside = fetch(blocks[len(blocks) // 2 - 1], head_weight), scored_lanes(counts)
+    weight, scored, *blocks = lax.optimization_barrier((*beside, *blocks))
     near = unpack(blocks, width)
-    far = with_fetch("core", near, move(near, 0, masks[-1], n))
-    far, scored = lax.optimization_barrier((far, scored_lanes(counts)))
-    owners = owners + [(s, m ^ masks[-1]) for s, m in owners]
-    weights = [fetched[place] for place in sorted(fetched, key=lambda place: FETCH[place])]
-    lines = row_stats(tuple(owners), near, far, weights)
+    far = move(near, 0, masks[-1], n)
+    lines = row_stats(n, tuple(owners), near, weight)
+    owners = [(s, m ^ masks[-1]) for s, m in owners]
+    lines = row_stats(n, tuple(owners), far, weight, lines)
     lines = lax.all_to_all(lines, "vocab", 0, 0, tiled=True)
     return finish(lines, scored, slots)
 

time: 29.6 us -> 29.4 us (level)
  waiting for transfers between devices: 2.38 us -> 1.35 us
  Pallas kernels: 5.35 us -> 6.14 us
    ppermute x8, waiting for transfers between devices: 2.38 us -> 1.35 us  [move(): lax.ppermute(block, 'vocab', [(i, (i + shift) % n ^ mask) for i in range(...]
    pallas_call x2 -> x3, Pallas kernels: 3.62 us -> 4.41 us  [the longest x1 2.35 us: fetch(): pl.pallas_call(fetch_kernel, out_shape=pltpu.VMEM(weight.shape, weight.dt...]
  transfers between devices with their start and end apart: 8 -> 8, of which waited for: 3 -> 2; matrix products, arithmetic and copies ran while one was open for 0% -> 0% of each run, Pallas kernels for 8% -> 12%
where the time goes in v1:
time: 29.4 us; the launch traced here: 29.2 us
  starting transfers between devices  10.7 us (36%)
  blocking collectives  9.67 us (33%)
  Pallas kernels  6.14 us (21%)
  between operations  1.36 us (5%)
  waiting for transfers between devices  1.35 us (5%)
    ppermute x8, starting transfers between devices, move(): lax.ppermute(block, 'vocab', [(i, (i + shift) % n ^ mask) for i in range(...  10.7 us
    all_to_all x1, blocking collectives, on_device(): lines = lax.all_to_all(lines, 'vocab', 0, 0, tiled=True)  9.67 us
    pallas_call x1, Pallas kernels, fetch(): pl.pallas_call(fetch_kernel, out_shape=pltpu.VMEM(weight.shape, weight.dt...  2.35 us
    pallas_call x2, Pallas kernels, row_stats(): pl.pallas_call(functools.partial(more_stats_kernel if more else stats_ker...  2.06 us
    ppermute x8, waiting for transfers between devices, move(): lax.ppermute(block, 'vocab', [(i, (i + shift) % n ^ mask) for i in range(...  1.35 us
    pallas_call x1, Pallas kernels, front(): pl.pallas_call(front_kernel, out_shape=pltpu.VMEM((HEAD, tiles * LANES),...  1.03 us
    pallas_call x1, Pallas kernels, finish(): pl.pallas_call(finish_kernel, out_shape=(jax.ShapeDtypeStruct((slots,), j...  0.6 us
  transfers between devices with their start and end apart: 8, of which 2 were waited for; matrix products, arithmetic and copies ran while one was open for 0% of the time, Pallas kernels for 12%

profile of v1, /device:TPU:0, one launch (start us, length us, event | category | flops | bytes accessed | tf_op | source)
XLA Modules:
  0.0 29.2 jit_solution(1904713705802421679)
XLA Ops:
  0.6 1.0 %norm_and_pack.1.refs_0_ = bf16[8,3072]{1,0:T(8,128)(2,1)S(1)} custom-call(bf16[16,2304]{1,0:T(8,128)(2,1)} %hidden_hbm.1, f32[2304]{0:T(1024)} %gain_hbm.1, s32[16]{0:T(128)} %targets_hbm.1), custom_call_target="tpu_custom_call" | custom-call | tf_op jit(solution)/shard_map/norm_and_pack/pallas_call | solution.py:82
  1.7 2.5 %collective-permute-start.1 = (bf16[8,3072]{1,0:T(8,128)(2,1)S(1)}, bf16[8,3072]{1,0:T(8,128)(2,1)S(1)}, u32[]{:S(2)}, u32[]{:S(2)}) collective-permute-start(bf16[8,3072]{1,0:T(8,128)(2,1)S(1)} %norm_and_pack.1.refs_0_), channel_id=1, source_target_pairs={{0,5},{1,4},{2,7},{3,6},{4,9},{5,8},{6,11},{7,10},{8,13},{9,12},{1... | collective-permute-start | bytes 147464 | tf_op jit(solution)/shard_map/ppermute | solution.py:32
  4.2 2.6 %collective-permute-start.2 = (bf16[8,3072]{1,0:T(8,128)(2,1)S(1)}, bf16[8,3072]{1,0:T(8,128)(2,1)S(1)}, u32[]{:S(2)}, u32[]{:S(2)}) collective-permute-start(bf16[8,3072]{1,0:T(8,128)(2,1)S(1)} %norm_and_pack.1.refs_0_), channel_id=1, source_target_pairs={{0,8},{1,9},{2,10},{3,11},{4,12},{5,13},{6,14},{7,15},{8,0},{9,1},... | collective-permute-start | bytes 147464 | tf_op jit(solution)/shard_map/ppermute | solution.py:32
  6.8 1.4 %collective-permute-start = (bf16[8,3072]{1,0:T(8,128)(2,1)S(1)}, bf16[8,3072]{1,0:T(8,128)(2,1)S(1)}, u32[]{:S(2)}, u32[]{:S(2)}) collective-permute-start(bf16[8,3072]{1,0:T(8,128)(2,1)S(1)} %norm_and_pack.1.refs_0_), channel_id=1, source_target_pairs={{0,13},{1,12},{2,15},{3,14},{4,1},{5,0},{6,3},{7,2},{8,5},{9,4},{1... | collective-permute-start | bytes 147464 | tf_op jit(solution)/shard_map/ppermute | solution.py:32
  8.2 1.2 %collective-permute-start.3 = (bf16[8,3072]{1,0:T(8,128)(2,1)S(1)}, bf16[8,3072]{1,0:T(8,128)(2,1)S(1)}, u32[]{:S(2)}, u32[]{:S(2)}) collective-permute-start(bf16[8,3072]{1,0:T(8,128)(2,1)S(1)} %norm_and_pack.1.refs_0_), channel_id=1, source_target_pairs={{0,3},{1,2},{2,1},{3,0},{4,7},{5,6},{6,5},{7,4},{8,11},{9,10},{10,... | collective-permute-start | bytes 147464 | tf_op jit(solution)/shard_map/ppermute | solution.py:32
  9.4 0.0 collective-permute-done.1.refs_1_
  9.4 0.7 %collective-permute-start.4 = (bf16[8,3072]{1,0:T(8,128)(2,1)S(1)}, bf16[8,3072]{1,0:T(8,128)(2,1)S(1)}, u32[]{:S(2)}, u32[]{:S(2)}) collective-permute-start(bf16[8,3072]{1,0:T(8,128)(2,1)S(1)} %collective-permute-done.1.refs_1_), channel_id=1, source_target_pairs={{0,3},{1,2},{2,1},{3,0},{4,7},{5,6},{6,5},{7,4},{8,11},{9,10},{10,... | collective-permute-start | bytes 147464 | tf_op jit(solution)/shard_map/ppermute | solution.py:32
  10.0 1.0 %collective-permute-done.2.refs_2_ = bf16[8,3072]{1,0:T(8,128)(2,1)S(1)} collective-permute-done((bf16[8,3072]{1,0:T(8,128)(2,1)S(1)}, bf16[8,3072]{1,0:T(8,128)(2,1)S(1)}, u32[]{:S(2)}, u32[]{:S(2)}) %collective-permute-start.2) | collective-permute-done | bytes 49184 | tf_op jit(solution)/shard_map/ppermute | solution.py:32
  11.1 1.3 %collective-permute-start.5 = (bf16[8,3072]{1,0:T(8,128)(2,1)S(1)}, bf16[8,3072]{1,0:T(8,128)(2,1)S(1)}, u32[]{:S(2)}, u32[]{:S(2)}) collective-permute-start(bf16[8,3072]{1,0:T(8,128)(2,1)S(1)} %collective-permute-done.2.refs_2_), channel_id=1, source_target_pairs={{0,3},{1,2},{2,1},{3,0},{4,7},{5,6},{6,5},{7,4},{8,11},{9,10},{10,... | collective-permute-start | bytes 147464 | tf_op jit(solution)/shard_map/ppermute | solution.py:32
  12.3 0.0 collective-permute-done.after_ref.refs_3_
  12.3 0.5 %collective-permute-start.6 = (bf16[8,3072]{1,0:T(8,128)(2,1)S(1)}, bf16[8,3072]{1,0:T(8,128)(2,1)S(1)}, u32[]{:S(2)}, u32[]{:S(2)}) collective-permute-start(bf16[8,3072]{1,0:T(8,128)(2,1)S(1)} %collective-permute-done.after_ref.refs_3_), channel_id=1, source_target_pairs={{0,3},{1,2},{2,1},{3,0},{4,7},{5,6},{6,5},{7,4},{8,11},{9,10},{10,... | collective-permute-start | bytes 147464 | tf_op jit(solution)/shard_map/ppermute | solution.py:32
  13.5 2.3 %fetch_weights.1.weight_ref = bf16[2304,1024]{1,0:T(8,128)(2,1)S(1)} custom-call(bf16[8,3072]{1,0:T(8,128)(2,1)S(1)} %collective-permute-done.after_ref.refs_3_, bf16[2304,1024]{1,0:T(8,128)(2,1)} %weight_ref.1), custom_call_target="tpu_custom_call" | custom-call | bytes 4718592 | tf_op jit(solution)/shard_map/fetch_weights/pallas_call | solution.py:106
  15.8 0.0 collective-permute-done.3.refs_4_
  15.8 0.0 collective-permute-done.4.refs_5_
  15.8 0.0 collective-permute-done.5.refs_6_
  15.9 0.0 collective-permute-done.6.refs_7_
  15.9 0.1 unpack.1.rows_in
  16.0 0.6 %collective-permute-start.7 = (bf16[80,2432]{1,0:T(8,128)(2,1)S(1)}, bf16[80,2432]{1,0:T(8,128)(2,1)S(1)}, u32[]{:S(2)}, u32[]{:S(2)}) collective-permute-start(bf16[80,2432]{1,0:T(8,128)(2,1)S(1)} %unpack.1.rows_in), channel_id=1, source_target_pairs={{0,1},{1,0},{2,3},{3,2},{4,5},{5,4},{6,7},{7,6},{8,9},{9,8},{10,11... | collective-permute-start | bytes 1167368 | tf_op jit(solution)/shard_map/ppermute | solution.py:32
  16.5 1.0 %row_stats.2.lines_in = f32[16,128]{1,0:T(8,128)S(1)} custom-call(bf16[80,2432]{1,0:T(8,128)(2,1)S(1)} %unpack.1.rows_in, bf16[2304,1024]{1,0:T(8,128)(2,1)S(1)} %fetch_weights.1.weight_ref), custom_call_target="tpu_custom_call" | custom-call | flops 398458880 | tf_op jit(solution)/shard_map/row_stats/pallas_call | solution.py:199
  17.6 0.3 %collective-permute-done.7.rows_in = bf16[80,2432]{1,0:T(8,128)(2,1)S(1)} collective-permute-done((bf16[80,2432]{1,0:T(8,128)(2,1)S(1)}, bf16[80,2432]{1,0:T(8,128)(2,1)S(1)}, u32[]{:S(2)}, u32[]{:S(2)}) %collective-permute-start.7) | collective-permute-done | bytes 389152 | tf_op jit(solution)/shard_map/ppermute | solution.py:32
  17.9 1.0 %row_stats.3 = f32[16,128]{1,0:T(8,128)S(1)} custom-call(bf16[80,2432]{1,0:T(8,128)(2,1)S(1)} %collective-permute-done.7.rows_in, bf16[2304,1024]{1,0:T(8,128)(2,1)S(1)} %fetch_weights.1.weight_ref, f32[16,128]{1,0:T(8,128)S(1)} %row_stats.2.lines_in), custom_call_target="tpu_custom_call", output_to_operand_aliasing={{}: (2, {})} | custom-call | flops 398458880 | tf_op jit(solution)/shard_map/row_stats/pallas_call | solution.py:199
  18.9 9.7 %all_to_all.11 = f32[16,1,128]{2,1,0:T(1,128)S(1)} all-to-all(f32[16,1,128]{2,1,0:T(1,128)S(1)} %bitcast.4), channel_id=1, replica_groups=mesh['req'=2,'vocab'=16] {'vocab'}, dimensions={0} | all-to-all | bytes 16384 | tf_op jit(solution)/shard_map/all_to_all | solution.py:274
  28.6 0.6 %finish.1 = (f32[16]{0:T(128)}, f32[16]{0:T(128)}) custom-call(f32[16,128]{1,0:T(8,128)S(1)} %bitcast.5, f32[8,128]{1,0:T(8,128)S(1)} %scored.1.scored_ref), custom_call_target="tpu_custom_call" | custom-call | tf_op jit(solution)/shard_map/finish/pallas_call | solution.py:248
  (1 shorter events, 0.0 us)
Async XLA Ops:
  1.7 7.7 %collective-permute-start.1 = (bf16[8,3072]{1,0:T(8,128)(2,1)S(1)}, bf16[8,3072]{1,0:T(8,128)(2,1)S(1)}, u32[]{:S(2)}, u32[]{:S(2)}) collective-permute-start(bf16[8,3072]{1,0:T(8,128)(2,1)S(1)} %norm_and_pack.1.refs_0_), channel_id=1, source_target_pairs={{0,5},{1,4},{2,7},{3,6},{4,9},{5,8},{6,11},{7,10},{8,13},{9,12},{1... | collective-permute-start | bytes 147464 | tf_op jit(solution)/shard_map/ppermute | solution.py:32
  4.2 6.9 %collective-permute-start.2 = (bf16[8,3072]{1,0:T(8,128)(2,1)S(1)}, bf16[8,3072]{1,0:T(8,128)(2,1)S(1)}, u32[]{:S(2)}, u32[]{:S(2)}) collective-permute-start(bf16[8,3072]{1,0:T(8,128)(2,1)S(1)} %norm_and_pack.1.refs_0_), channel_id=1, source_target_pairs={{0,8},{1,9},{2,10},{3,11},{4,12},{5,13},{6,14},{7,15},{8,0},{9,1},... | collective-permute-start | bytes 147464 | tf_op jit(solution)/shard_map/ppermute | solution.py:32
  6.8 5.6 %collective-permute-start = (bf16[8,3072]{1,0:T(8,128)(2,1)S(1)}, bf16[8,3072]{1,0:T(8,128)(2,1)S(1)}, u32[]{:S(2)}, u32[]{:S(2)}) collective-permute-start(bf16[8,3072]{1,0:T(8,128)(2,1)S(1)} %norm_and_pack.1.refs_0_), channel_id=1, source_target_pairs={{0,13},{1,12},{2,15},{3,14},{4,1},{5,0},{6,3},{7,2},{8,5},{9,4},{1... | collective-permute-start | bytes 147464 | tf_op jit(solution)/shard_map/ppermute | solution.py:32
  8.2 7.7 %collective-permute-start.3 = (bf16[8,3072]{1,0:T(8,128)(2,1)S(1)}, bf16[8,3072]{1,0:T(8,128)(2,1)S(1)}, u32[]{:S(2)}, u32[]{:S(2)}) collective-permute-start(bf16[8,3072]{1,0:T(8,128)(2,1)S(1)} %norm_and_pack.1.refs_0_), channel_id=1, source_target_pairs={{0,3},{1,2},{2,1},{3,0},{4,7},{5,6},{6,5},{7,4},{8,11},{9,10},{10,... | collective-permute-start | bytes 147464 | tf_op jit(solution)/shard_map/ppermute | solution.py:32
  9.4 6.5 %collective-permute-start.4 = (bf16[8,3072]{1,0:T(8,128)(2,1)S(1)}, bf16[8,3072]{1,0:T(8,128)(2,1)S(1)}, u32[]{:S(2)}, u32[]{:S(2)}) collective-permute-start(bf16[8,3072]{1,0:T(8,128)(2,1)S(1)} %collective-permute-done.1.refs_1_), channel_id=1, source_target_pairs={{0,3},{1,2},{2,1},{3,0},{4,7},{5,6},{6,5},{7,4},{8,11},{9,10},{10,... | collective-permute-start | bytes 147464 | tf_op jit(solution)/shard_map/ppermute | solution.py:32
  11.1 4.8 %collective-permute-start.5 = (bf16[8,3072]{1,0:T(8,128)(2,1)S(1)}, bf16[8,3072]{1,0:T(8,128)(2,1)S(1)}, u32[]{:S(2)}, u32[]{:S(2)}) collective-permute-start(bf16[8,3072]{1,0:T(8,128)(2,1)S(1)} %collective-permute-done.2.refs_2_), channel_id=1, source_target_pairs={{0,3},{1,2},{2,1},{3,0},{4,7},{5,6},{6,5},{7,4},{8,11},{9,10},{10,... | collective-permute-start | bytes 147464 | tf_op jit(solution)/shard_map/ppermute | solution.py:32
  12.3 3.5 %collective-permute-start.6 = (bf16[8,3072]{1,0:T(8,128)(2,1)S(1)}, bf16[8,3072]{1,0:T(8,128)(2,1)S(1)}, u32[]{:S(2)}, u32[]{:S(2)}) collective-permute-start(bf16[8,3072]{1,0:T(8,128)(2,1)S(1)} %collective-permute-done.after_ref.refs_3_), channel_id=1, source_target_pairs={{0,3},{1,2},{2,1},{3,0},{4,7},{5,6},{6,5},{7,4},{8,11},{9,10},{10,... | collective-permute-start | bytes 147464 | tf_op jit(solution)/shard_map/ppermute | solution.py:32
  16.0 1.9 %collective-permute-start.7 = (bf16[80,2432]{1,0:T(8,128)(2,1)S(1)}, bf16[80,2432]{1,0:T(8,128)(2,1)S(1)}, u32[]{:S(2)}, u32[]{:S(2)}) collective-permute-start(bf16[80,2432]{1,0:T(8,128)(2,1)S(1)} %unpack.1.rows_in), channel_id=1, source_target_pairs={{0,1},{1,0},{2,3},{3,2},{4,5},{5,4},{6,7},{7,6},{8,9},{9,8},{10,11... | collective-permute-start | bytes 1167368 | tf_op jit(solution)/shard_map/ppermute | solution.py:32
